TPU v7x, 128 devices: a whole 4x4x4 slice. The times are simulated.
128 devices in a mesh: dp: 64 (over z_hi, y, x, core), tensor: 2 (over z_lo).
Axes of the slice: x: 4, y: 4, z: 4 (z_hi: 2, z_lo: 2; z = z_hi * 2 + z_lo), core: 2. Of those that a mesh axis runs over, the one named last changes fastest.
Arguments:
- tokens: bfloat16 [32768, 1024], P('dp'), may hold values from -16 to 16
- gain_one: float32 [1024], replicated, may hold values from 0.5 to 1.5
- shift_one: float32 [1024], replicated, may hold values from -1.25 to 1.25
- qkv_weight: bfloat16 [1024, 3, 1024], P(None, None, 'tensor'), may hold values from -0.1875 to 0.1875
- qv_bias: bfloat16 [2, 1024], P(None, 'tensor'), may hold values from -1.75 to 1.75
- out_weight: bfloat16 [1024, 1024], P('tensor'), may hold values from -0.375 to 0.375
- out_bias: bfloat16 [1024], replicated, may hold values from -1.75 to 1.75
- gain_two: float32 [1024], replicated, may hold values from 0.5 to 1.5
- shift_two: float32 [1024], replicated, may hold values from -1.25 to 1.25
- up_weight: bfloat16 [1024, 4096], P(None, 'tensor'), may hold values from -0.1875 to 0.1875
- up_bias: bfloat16 [4096], P('tensor'), may hold values from -1.75 to 1.75
- down_weight: bfloat16 [4096, 1024], P('tensor'), may hold values from -0.09375 to 0.09375
- down_bias: bfloat16 [1024], replicated, may hold values from -1.75 to 1.75
- cotangent: bfloat16 [32768, 1024], P('dp'), may hold values from -16 to 16
Outputs:
- block_out: bfloat16 [32768, 1024], P('dp')
- token_grad: float32 [32768, 1024], P('dp')
- grad_gain_one: float32 [1024], P('dp')
- grad_shift_one: float32 [1024], P('dp')
- grad_qkv_weight: float32 [1024, 3, 1024], P('dp', None, 'tensor')
- grad_qv_bias: float32 [2, 1024], P(None, 'tensor')
- grad_out_weight: float32 [1024, 1024], P('tensor', 'dp')
- grad_out_bias: float32 [1024], P('dp')
- grad_gain_two: float32 [1024], P('dp')
- grad_shift_two: float32 [1024], P('dp')
- grad_up_weight: float32 [1024, 4096], P('dp', 'tensor')
- grad_up_bias: float32 [4096], P('tensor')
- grad_down_weight: float32 [4096, 1024], P('tensor', 'dp')
- grad_down_bias: float32 [1024], P('dp')
All inputs are finite; a program needn't handle non-finite values.
Results may differ from a plain program's by a relative error of at most 0.01.
Values sent between devices are 32-bit elements; how exact they have to be, the bound alone decides.
A program may use at most 256 MiB of HBM per device.

v0:
```python
import functools
import math

import jax
import jax.numpy as jnp
from jax import lax
from jax.experimental import pallas as pl
from jax.experimental.pallas import tpu as pltpu
from jax.sharding import PartitionSpec as P

DH = 64
epsilon = 1e-05
bf16 = jnp.bfloat16
f32 = jnp.float32


def layer_norm_parts(values):
    centre = jnp.mean(values, axis=-1, keepdims=True)
    centered = values - centre
    spread = jnp.mean(centered * centered, axis=-1, keepdims=True)
    r = lax.rsqrt(spread + epsilon)
    return centered * r, r


def layer_norm_back(grad, n, r, gain):
    e = grad * gain
    mean_e = jnp.mean(e, axis=-1, keepdims=True)
    mean_en = jnp.mean(e * n, axis=-1, keepdims=True)
    return (
        r * (e - mean_e - n * mean_en),
        jnp.sum(grad * n, axis=0),
        jnp.sum(grad, axis=0),
    )


GC, GA = 0.7978845608028654, 0.044715


def gelu_both(v):
    square = v * v
    h = 0.5 + 0.5 * jnp.tanh(v * (GC + GC * GA * square))
    value = v * h
    slope = h + (value * (1.0 - h)) * (2.0 * GC + 6.0 * GC * GA * square)
    return value, slope


NT = (((1,), (1,)), ((), ()))
TN = (((0,), (0,)), ((), ()))
NN = (((1,), (0,)), ((), ()))


def dot(a, b, dims=NN):
    return lax.dot_general(a, b, dims, preferred_element_type=f32)


def half_lanes(block, side):
    lane = lax.broadcasted_iota(jnp.int32, block.shape, 1)
    return jnp.where((lane >= 64) == (side == 1), block, jnp.zeros_like(block))


def fill_distance(ref):
    row = lax.broadcasted_iota(jnp.int32, ref.shape, 0)
    col = lax.broadcasted_iota(jnp.int32, ref.shape, 1)
    ref[...] = jnp.where(row >= col, (row - col).astype(f32), 1e30)


def attend_pair(q, k, v, slopes, distance):
    outs, lses = [], []
    scaled = q * 0.125
    for side in range(2):
        out, lse = [], []
        for rows, keys in ((slice(0, 256), 256), (slice(256, 512), 512)):
            s = dot(half_lanes(scaled[rows], side), k[:keys], NT) - slopes[side] * distance[rows, :keys]
            top = jnp.max(s, axis=-1, keepdims=True)
            e = jnp.exp(s - top)
            total = jnp.sum(e, axis=-1, keepdims=True)
            out.append(dot((e * (1.0 / total)).astype(bf16), v[:keys]))
            lse.append(top + jnp.log(total))
        outs.append(jnp.concatenate(out, axis=0))
        lses.append(jnp.concatenate(lse, axis=0))
    lane = lax.broadcasted_iota(jnp.int32, outs[0].shape, 1)
    return jnp.where(lane < 64, outs[0], outs[1]).astype(bf16), lses


def attend_back_pair(q, k, v, lse, g, slopes, distance):
    dqs, dks, dvs = [], [], []
    scaled = q * 0.125
    for side in range(2):
        dq, dk, dv = [], [], []
        for rows, keys in ((slice(0, 256), 256), (slice(256, 512), 512)):
            s = dot(half_lanes(scaled[rows], side), k[:keys], NT) - slopes[side] * distance[rows, :keys]
            a = jnp.exp(s - lse[side][rows])
            w = dot(half_lanes(g[rows], side), v[:keys], NT)
            inner = jnp.sum(a * w, axis=-1, keepdims=True)
            ds = (a * (w - inner)).astype(bf16)
            dv.append(dot(a.astype(bf16), g[rows], TN))
            dq.append(dot(ds, k[:keys]) * 0.125)
            dk.append(dot(ds, q[rows], TN) * 0.125)
        dqs.append(jnp.concatenate(dq, axis=0))
        for parts, total in ((dk, dks), (dv, dvs)):
            total.append(jnp.concatenate([parts[0] + parts[1][:256], parts[1][256:]], axis=0))
    lane = lax.broadcasted_iota(jnp.int32, dqs[0].shape, 1)
    return [jnp.where(lane < 64, p[0], p[1]).astype(bf16) for p in (dqs, dks, dvs)]


def unit_block(n2, cot, up, up_dims, bias, down):
    value, slope = gelu_both(dot(n2, up, up_dims) + bias)
    active = value.astype(bf16)
    gh = (dot(cot, down, NT) * slope).astype(bf16)
    back_dims = NT if up_dims is NN else NN
    return active, gh, dot(active, down), dot(gh, up, back_dims)


MESH = pl.DeviceIdType.MESH


def forward_kernel(
    slopes,
    tokens,
    rows_ref,
    low_rows,
    wqkv,
    wout,
    up_any,
    down_any,
    cot_any,
    n1_out,
    q_out,
    k_out,
    v_out,
    att_out,
    lse_ref,
    woth_out,
    units_any,
    n2_out,
    act_out,
    gh_out,
    gb_ref,
    out_ref,
    grad_ref,
    branch_ref,
    vec_ref,
    n1_ref,
    q_ref,
    k_ref,
    v_ref,
    att_ref,
    woth_ref,
    n2_ref,
    act_ref,
    gh_ref,
    bias_rows,
    bias_piece,
    piece,
    turned,
    distance,
    got,
    got_bias,
    bias_out,
    up,
    down,
    cot,
    feed_ref,
    gn_ref,
    hsend,
    hrecv,
    usend,
    urecv,
    bsend,
    brecv,
    lsem,
    fsem,
    osem,
):
    dp, tensor = lax.axis_index("dp"), lax.axis_index("tensor")
    core, x, y, zh = dp % 2, (dp // 2) % 4, (dp // 8) % 4, dp // 32
    z = zh * 2 + tensor
    ring = jnp.where(core == 0, x, y)

    def device(nx, ny, nz, nc):
        return ((((nz // 2) * 4 + ny) * 4 + nx) * 2 + nc, nz % 2)

    def on_ring(r):
        return device(jnp.where(core == 0, r, x), jnp.where(core == 0, y, r), z, core)

    z_plus, z_minus = device(x, y, (z + 1) % 4, core), device(x, y, (z + 3) % 4, core)
    r_plus, r_minus = on_ring((ring + 1) % 4), on_ring((ring + 3) % 4)
    partner = device(x, y, z, 1 - core)
    barrier = pltpu.get_barrier_semaphore()
    for d in (z_plus, z_minus, r_plus, r_minus, partner):
        pl.semaphore_signal(barrier, inc=1, device_id=d, device_id_type=MESH)
    local = [
        pltpu.make_async_copy(a, b, lsem.at[k])
        for k, (a, b) in enumerate(((up_any, up), (down_any, down), (cot_any, cot)))
    ]
    for c in local:
        c.start()
    pid, fid = 4 * core + ring, 4 * core + (ring + 2) % 4
    for m in range(3):
        turned[...] = wqkv[m, :, pl.ds(pl.multiple_of(pid // 2 * 128, 128), 128)].T
        side = pl.ds(pl.multiple_of(pid % 2 * 64, 64), 64)
        piece[0, m * 64 : m * 64 + 64, :] = turned[side, :].astype(f32)
    piece[0, 192:256, :] = wout[pl.ds(pl.multiple_of(pid * 64, 64), 64), :].astype(f32)
    bias_rows[...] = low_rows[...].astype(f32)
    for p in range(8):
        q_part = bias_rows[4:5, 64 * p : 64 * p + 64]
        v_part = bias_rows[4:5, 512 + 64 * p : 576 + 64 * p]
        bias_piece[p : p + 1, :] = jnp.concatenate([q_part, q_part, v_part, v_part], axis=1)
        bias_piece[8 + p : 9 + p, :] = bias_rows[2 + p // 4 : 3 + p // 4, p % 4 * 256 : p % 4 * 256 + 256]
    pl.semaphore_wait(barrier, 5)

    def place(u, slot, sub):
        at = pl.ds(sub * 64, 64)
        return got.at[slot, at] if u == 0 else units_any.at[u - 1, slot, at]

    def move(u, src, slot, sub, way, target):
        send = hsend.at[slot, sub, way] if u == 0 else usend.at[u - 1, slot, sub, way]
        recv = hrecv.at[slot, sub] if u == 0 else urecv.at[u - 1, slot, sub]
        return pltpu.make_async_remote_copy(
            src_ref=src,
            dst_ref=place(u, slot, sub),
            send_sem=send,
            recv_sem=recv,
            device_id=target,
            device_id_type=MESH,
        )

    started = [[], [], []]

    def begin(u, src, slot, sub, target):
        c = move(u, src, slot, sub, 0, target)
        c.start()
        started[u].append(c)

    def arrived(u, slot, sub):
        move(u, place(u, slot, sub), slot, sub, 0, partner).wait_recv()

    bias_move = pltpu.make_async_remote_copy(
        src_ref=bias_piece, dst_ref=got_bias, send_sem=bsend, recv_sem=brecv, device_id=z_plus, device_id_type=MESH
    )
    outgoing = []

    def leave(k, src, dst):
        c = pltpu.make_async_copy(src, dst, osem.at[k])
        c.start()
        outgoing.append(c)

    def to_z(u, src, slot):
        for sub in (0, 2, 1, 3):
            begin(u, piece.at[src, pl.ds(sub * 64, 64)], slot, sub, z_plus if sub < 2 else z_minus)

    to_z(0, 0, 0)
    bias_move.start()
    fill_distance(distance)

    def own_came(u, subs):
        for sub in subs:
            arrived(u, 0, sub)
            begin(u, place(u, 0, sub), 1, sub, r_plus)
            begin(u, place(u, 0, sub), 2, sub, r_minus)
        for sub in subs:
            begin(u, place(u, 0, sub), 4, sub, partner)

    def next_came(u, low, high):
        arrived(u, 1, low)
        if low < 2 and u < 2:
            begin(u, place(u, 1, low), 3, low, r_plus)
        begin(u, place(u, 1, low), 5, low, partner)
        arrived(u, 2, high)
        if high >= 2 and u < 2:
            begin(u, place(u, 2, high), 3, high, r_minus)
        begin(u, place(u, 2, high), 6, high, partner)

    def far_came(u, subs):
        for sub in subs:
            arrived(u, 3, sub)
            begin(u, place(u, 3, sub), 7, sub, partner)

    def swapped(u, slots):
        for slot in slots:
            for sub in range(4):
                arrived(u, slot, sub)

    pump = [lambda u=u, f=f: f(u) for u in range(3) for f in (
        lambda u: own_came(u, (0, 2)),
        lambda u: own_came(u, (1, 3)),
        lambda u: next_came(u, 0, 2),
        lambda u: next_came(u, 2, 0),
        lambda u: next_came(u, 1, 3),
        lambda u: next_came(u, 3, 1),
        lambda u: far_came(u, (0, 2)),
        lambda u: far_came(u, (1, 3)),
        lambda u: swapped(u, range(4, 8) if u < 2 else (4, 5, 6)),
    )]

    def norm_one(r, carry):
        at = pl.ds(r * 128, 128)
        n, _ = layer_norm_parts(tokens[at, :].astype(f32))
        n1_ref[at, :] = (n * rows_ref[0:1, :] + rows_ref[1:2, :]).astype(bf16)
        return carry

    lax.fori_loop(0, 4, norm_one, 0)
    n1 = n1_ref[...]
    q_ref[0] = (dot(n1, wqkv[0]) + bias_rows[4:5, :512]).astype(bf16)
    k_ref[0] = dot(n1, wqkv[1]).astype(bf16)
    v_ref[0] = (dot(n1, wqkv[2]) + bias_rows[4:5, 512:]).astype(bf16)
    leave(0, n1_ref, n1_out)
    for c in local:
        c.wait()
    piece[1] = up[:, pl.ds(pl.multiple_of(pid * 256, 256), 256)].T.astype(f32)
    piece[2] = down[pl.ds(pl.multiple_of(pid * 256, 256), 256), :].astype(f32)
    piece[3] = down[pl.ds(pl.multiple_of(fid * 256, 256), 256), :].astype(f32)
    to_z(1, 1, 0)
    to_z(2, 2, 0)
    to_z(2, 3, 3)

    lse_ref[...] = jnp.zeros_like(lse_ref)

    def put_lse(head, pair):
        lane = lax.broadcasted_iota(jnp.int32, lse_ref.shape, 1)
        for side in range(2):
            lse_ref[...] = jnp.where(lane == head + side, pair[side], lse_ref[...])

    def own_pair(p, carry):
        lanes = pl.ds(pl.multiple_of(p * 128, 128), 128)
        out, lse = attend_pair(
            q_ref[0, :, lanes], k_ref[0, :, lanes], v_ref[0, :, lanes], (slopes[2 * p], slopes[2 * p + 1]), distance
        )
        att_ref[0, :, lanes] = out
        put_lse(2 * p, lse)
        return carry

    lax.fori_loop(0, 1, own_pair, 0)
    pump[0]()
    lax.fori_loop(1, 4, own_pair, 0)
    pump[1]()
    pump[2]()
    feed_ref[...] = dot(att_ref[0], wout[...])
    for k in range(3, 6):
        pump[k]()
    bias_move.wait()
    ring_other = jnp.where(core == 0, y, x)
    for k, o in enumerate((0, 3, 1, 2)):
        for slot, pid in ((k, 4 * core + (ring + o) % 4), (k + 4, 4 * (1 - core) + (ring_other + o) % 4)):
            bias_out[slot : slot + 1, :] = got_bias[pl.ds(pid, 1), :]
            bias_out[8 + slot : 9 + slot, :] = got_bias[pl.ds(8 + pid, 1), :]

    def other_pair(p, carry):
        lanes = pl.ds(pl.multiple_of(p * 128, 128), 128)
        for m in range(4):
            for side in range(2):
                at = pl.ds(pl.multiple_of(p * 128 + side * 64, 64), 64)
                woth_ref[m, at, :] = got[2 * p + side, m * 64 : m * 64 + 64, :].astype(bf16)
        low, high = bias_out[pl.ds(2 * p, 1), :], bias_out[pl.ds(2 * p + 1, 1), :]
        parts = []
        for m in range(3):
            parts.append(dot(n1_ref[...], woth_ref[m, lanes, :], NT))
        lane = lax.broadcasted_iota(jnp.int32, (1, 128), 1)
        q = (parts[0] + jnp.where(lane < 64, low[:, :128], high[:, :128])).astype(bf16)
        k = parts[1].astype(bf16)
        v = (parts[2] + jnp.where(lane < 64, low[:, 128:], high[:, 128:])).astype(bf16)
        q_ref[1, :, lanes] = q
        k_ref[1, :, lanes] = k
        v_ref[1, :, lanes] = v
        out, lse = attend_pair(q, k, v, (slopes[8 + 2 * p], slopes[9 + 2 * p]), distance)
        att_ref[1, :, lanes] = out
        put_lse(8 + 2 * p, lse)
        return carry

    lax.fori_loop(0, 1, other_pair, 0)
    for k in (9, 6, 7, 8, 10):
        pump[k]()
    lax.fori_loop(1, 4, other_pair, 0)
    pump[11]()
    feed_ref[...] += dot(att_ref[1], woth_ref[3])
    pump[12]()

    def norm_two(r, carry):
        at = pl.ds(r * 128, 128)
        middle = tokens[at, :].astype(f32) + (feed_ref[at, :] + bias_rows[0:1, :])
        grad_ref[at, :] = middle
        n, _ = layer_norm_parts(middle)
        n2_ref[at, :] = (n * rows_ref[2:3, :] + rows_ref[3:4, :]).astype(bf16)
        return carry

    lax.fori_loop(0, 4, norm_two, 0)
    leave(1, q_ref, q_out)
    leave(2, k_ref, k_out)
    leave(3, v_ref, v_out)
    leave(4, att_ref, att_out)
    leave(5, woth_ref, woth_out)
    leave(6, n2_ref, n2_out)
    pump[13]()
    pump[14]()
    feed_ref[...] = jnp.zeros_like(feed_ref)
    gn_ref[...] = jnp.zeros_like(gn_ref)

    def unit_step(i, carry):
        lanes = pl.ds(pl.multiple_of(i * 512, 512), 512)
        within = pl.ds(pl.multiple_of(i % 2 * 512, 512), 512)
        where = (pl.ds(2 + i // 2, 1), within)
        active, gh, feed, gn = unit_block(
            n2_ref[...], cot[...], up[:, lanes], NN, bias_rows[where], down[lanes, :]
        )
        act_ref[:, lanes] = active
        gh_ref[:, lanes] = gh
        gb_ref[pl.ds(i // 2, 1), within] = jnp.sum(gh.astype(f32), axis=0, keepdims=True)
        feed_ref[...] += feed
        gn_ref[...] += gn
        return carry

    def fetch(number, slots):
        return [
            pltpu.make_async_copy(
                units_any.at[k, slot], got.at[4 * number + 2 * k + n], fsem.at[number, 2 * k + n]
            )
            for k in range(2)
            for n, slot in enumerate(slots)
        ]

    def other_step(number, slots):
        for c in fetch(number, slots):
            c.wait()
        up_two, down_two = (
            jnp.concatenate([got[4 * number + 2 * k].astype(bf16), got[4 * number + 2 * k + 1].astype(bf16)], axis=0)
            for k in range(2)
        )
        bias = jnp.concatenate([bias_out[8 + slot : 9 + slot, :] for slot in slots], axis=1)
        _, _, feed, gn = unit_block(n2_ref[...], cot[...], up_two, NT, bias, down_two)
        feed_ref[...] += feed
        gn_ref[...] += gn

    def bring(number, slots):
        for c in fetch(number, slots):
            c.start()

    lax.fori_loop(0, 1, unit_step, 0)
    for k in (18, 15, 16):
        pump[k]()
    lax.fori_loop(1, 2, unit_step, 0)
    for k in (19, 17):
        pump[k]()
    lax.fori_loop(2, 3, unit_step, 0)
    pump[20]()
    pump[21]()
    lax.fori_loop(3, 4, unit_step, 0)
    leave(7, act_ref, act_out)
    leave(8, gh_ref, gh_out)
    for c in started[0]:
        c.wait_send()
    swapped(2, (4,))
    bring(0, (0, 4))
    pump[22]()
    pump[24]()
    pump[25]()
    swapped(2, (7,))
    bring(1, (3, 7))
    other_step(0, (0, 4))
    pump[23]()
    bring(0, (1, 2))
    other_step(1, (3, 7))
    swapped(2, (5, 6))
    bring(1, (5, 6))
    other_step(0, (1, 2))
    other_step(1, (5, 6))
    vec_ref[...] = jnp.zeros_like(vec_ref)

    def rows_of(r, carry):
        at = pl.ds(pl.multiple_of(r * 64, 64), 64)
        middle = grad_ref[at, :]
        cotangent = cot[at, :].astype(f32)
        out_ref[at, :] = (middle + (feed_ref[at, :] + bias_rows[1:2, :])).astype(bf16)
        n, root = layer_norm_parts(middle)
        back, ggain, gshift = layer_norm_back(gn_ref[at, :], n, root, rows_ref[2:3, :])
        whole = cotangent + back
        rounded = whole.astype(bf16)
        grad_ref[at, :] = whole
        branch_ref[at, :] = rounded
        vec_ref[0:1, :] += ggain[None]
        vec_ref[1:2, :] += gshift[None]
        vec_ref[2:3, :] += jnp.sum(rounded.astype(f32), axis=0, keepdims=True)
        vec_ref[3:4, :] += jnp.sum(cotangent, axis=0, keepdims=True)
        return carry

    lax.fori_loop(0, 8, rows_of, 0)
    for c in started[1] + started[2]:
        c.wait_send()
    for c in outgoing:
        c.wait()


def forward(slopes, tokens, rows, low_rows, wqkv, wout, up, down, cot):
    length, width = tokens.shape
    local, units = wout.shape[0], up.shape[1]
    vmem = pl.BlockSpec(memory_space=pltpu.VMEM)
    hbm = pl.BlockSpec(memory_space=pl.ANY)

    def out(shape, kind):
        return jax.ShapeDtypeStruct(shape, kind)

    return pl.pallas_call(
        forward_kernel,
        in_specs=[pl.BlockSpec(memory_space=pltpu.SMEM)] + [vmem] * 5 + [hbm] * 3,
        out_specs=[hbm] * 5 + [vmem] + [hbm] * 5 + [vmem] * 5,
        out_shape=[
            out((length, width), bf16),
            out((2, length, local), bf16),
            out((2, length, local), bf16),
            out((2, length, local), bf16),
            out((2, length, local), bf16),
            out((length, 128), f32),
            out((4, local, width), bf16),
            out((2, 8, 256, width), f32),
            out((length, width), bf16),
            out((length, units), bf16),
            out((length, units), bf16),
            out((2, width), f32),
            out((length, width), bf16),
            out((length, width), f32),
            out((length, width), bf16),
            out((8, width), f32),
        ],
        scratch_shapes=[
            pltpu.VMEM((length, width), bf16),
            *[pltpu.VMEM((2, length, local), bf16)] * 4,
            pltpu.VMEM((4, local, width), bf16),
            pltpu.VMEM((length, width), bf16),
            pltpu.VMEM((length, units), bf16),
            pltpu.VMEM((length, units), bf16),
            pltpu.VMEM((8, width), f32),
            pltpu.VMEM((16, 256), f32),
            pltpu.VMEM((4, 256, width), f32),
            pltpu.VMEM((128, width), bf16),
            pltpu.VMEM((length, length), f32),
            pltpu.VMEM((8, 256, width), f32),
            pltpu.VMEM((16, 256), f32),
            pltpu.VMEM((16, 256), f32),
            pltpu.VMEM((width, units), bf16),
            pltpu.VMEM((units, width), bf16),
            pltpu.VMEM((length, width), bf16),
            pltpu.VMEM((length, width), f32),
            pltpu.VMEM((length, width), f32),
            pltpu.SemaphoreType.DMA((8, 4, 1)),
            pltpu.SemaphoreType.DMA((8, 4)),
            pltpu.SemaphoreType.DMA((2, 8, 4, 1)),
            pltpu.SemaphoreType.DMA((2, 8, 4)),
            pltpu.SemaphoreType.DMA,
            pltpu.SemaphoreType.DMA,
            pltpu.SemaphoreType.DMA((3,)),
            pltpu.SemaphoreType.DMA((2, 4)),
            pltpu.SemaphoreType.DMA((9,)),
        ],
        compiler_params=pltpu.CompilerParams(
            collective_id=1, has_side_effects=True, vmem_limit_bytes=62 * 2**20
        ),
    )(slopes, tokens, rows, low_rows, wqkv, wout, up, down, cot)


W = 512
OFFSETS = (0, 1, 2, 3, 4, 5, 6)
SLOTS = 4


def ring_scratch(nb):
    return [
        pltpu.VMEM((2, 512, 512), bf16),
        pltpu.VMEM((SLOTS, 4, 128, W), f32),
        pltpu.VMEM((2, 4, 128, W), f32),
        pltpu.VMEM((SLOTS, 4, 128, W), f32),
        pltpu.VMEM((nb, 64, W), f32),
        pltpu.VMEM((nb, 64, W), f32),
        pltpu.VMEM((nb, 128, W), f32),
        pltpu.VMEM((nb, 128, W), f32),
        pltpu.VMEM((SLOTS, 4, 32, W), f32),
        pltpu.VMEM((nb, 16, W), f32),
        pltpu.VMEM((nb, 16, W), f32),
        pltpu.VMEM((nb, 32, W), f32),
        pltpu.VMEM((nb, 32, W), f32),
        pltpu.VMEM((SLOTS, 2, 16, W), f32),
        pltpu.VMEM((nb, 16, W), f32),
        pltpu.SemaphoreType.DMA((10, nb)),
        pltpu.SemaphoreType.DMA((10, nb)),
        pltpu.SemaphoreType.REGULAR,
    ]


class Ring:
    def __init__(self, blocks, narrow, scratch):
        self.blocks, self.narrow = blocks, narrow
        (
            self.lt, self.s, self.other, self.crecv, self.p1, self.m1, self.p2, self.m2, self.t,
            self.q1, self.r1, self.q2, self.r2, self.u, self.zrecv, self.ssem, self.rsem, self.credit,
        ) = scratch
        dp = lax.axis_index("dp")
        core = dp % 2
        x, y, zh = (dp // 2) % 4, (dp // 8) % 4, dp // 32
        self.core, self.zh = core, zh
        a = jnp.where(core == 0, x, y)
        b = jnp.where(core == 0, y, x)
        self.a, self.b = a, b

        def device(na, nb):
            nx = jnp.where(core == 0, na, nb)
            ny = jnp.where(core == 0, nb, na)
            return ((zh * 4 + ny) * 4 + nx) * 2 + core

        self.ap, self.am, self.a2 = (a + 1) % 4, (a + 3) % 4, (a + 2) % 4
        self.bp, self.bm, self.b2 = (b + 1) % 4, (b + 3) % 4, (b + 2) % 4
        self.to_ap, self.to_am = device(self.ap, b), device(self.am, b)
        self.to_bp, self.to_bm = device(a, self.bp), device(a, self.bm)
        self.to_a2, self.to_b2 = device(self.a2, b), device(a, self.b2)
        self.partner = dp + 1 - 2 * core
        self.across = dp + 32 - 64 * zh
        barrier = pltpu.get_barrier_semaphore()
        everyone = (
            self.partner, self.to_ap, self.to_am, self.to_bp, self.to_bm, self.to_a2, self.to_b2, self.across,
        )
        for d in everyone:
            pl.semaphore_signal(barrier, inc=1, device_id={"dp": d}, device_id_type=MESH)
        self.barrier = barrier

    def enter(self):
        pl.semaphore_wait(self.barrier, 8)

    def copies(self, stage, i, wide):
        def copy(kind, src, dst, d):
            if not wide:
                lanes = (slice(None),) * (len(src.shape) - 1) + (pl.ds(0, 128),)
                src, dst = src.at[lanes], dst.at[lanes]
            return pltpu.make_async_remote_copy(
                src_ref=src,
                dst_ref=dst,
                send_sem=self.ssem.at[kind, i],
                recv_sem=self.rsem.at[kind, i],
                device_id={"dp": d},
                device_id_type=MESH,
            )

        k = i % SLOTS
        if stage == 0:
            return [copy(0, self.other.at[i % 2], self.crecv.at[k], self.partner)]
        if stage == 1:
            return [
                copy(1, self.s.at[k, self.a2, pl.ds(0, 64)], self.p1.at[i], self.to_ap),
                copy(2, self.s.at[k, self.a2, pl.ds(64, 64)], self.m1.at[i], self.to_am),
            ]
        if stage == 2:
            return [
                copy(3, self.s.at[k, self.ap], self.p2.at[i], self.to_ap),
                copy(4, self.s.at[k, self.am], self.m2.at[i], self.to_am),
            ]
        if stage == 3:
            return [
                copy(5, self.t.at[k, self.b2, pl.ds(0, 16)], self.q1.at[i], self.to_bp),
                copy(6, self.t.at[k, self.b2, pl.ds(16, 16)], self.r1.at[i], self.to_bm),
            ]
        if stage == 4:
            return [
                copy(7, self.t.at[k, self.bp], self.q2.at[i], self.to_bp),
                copy(8, self.t.at[k, self.bm], self.r2.at[i], self.to_bm),
            ]
        return [copy(9, self.u.at[k, 1 - self.zh], self.zrecv.at[i], self.across)]

    def each(self, stage, i, act):
        few = functools.reduce(jnp.logical_or, [i == n for n in self.narrow])
        for wide in (True, False):
            @pl.when(few != wide)
            def _(wide=wide):
                for c in self.copies(stage, i, wide):
                    act(c)

    def start(self, stage, i):
        self.each(stage, i, lambda c: c.start())

    def wait(self, stage, i):
        self.each(stage, i, lambda c: c.wait())

    @staticmethod
    def slabs(part):
        for k in range(8):
            yx, c = k // 2, k % 2
            half, row = part // 4, part % 4
            first, second = (yx, row) if c == 0 else (row, yx)
            yield c, first, (second * 2 + half) * 16, k * 16

    def turn(self, left):
        for part in range(8):
            flipped = left[:, part * 128 : (part + 1) * 128].T
            for c, first, at, row in self.slabs(part):
                self.lt[c, first * 128 + at : first * 128 + at + 16, :] = flipped[row : row + 16, :]

    def make_product(self, i, right):
        own = dot(self.lt[self.core], right)
        away = dot(self.lt[1 - self.core], right)
        for chunk in range(4):
            self.s[i % SLOTS, chunk] = own[chunk * 128 : (chunk + 1) * 128]
            self.other[i % 2, chunk] = away[chunk * 128 : (chunk + 1) * 128]

    def make_small(self, i, small):
        k = i % SLOTS
        for part in range(8):
            flipped = small[:, part * 128 : (part + 1) * 128].T
            for c, first, at, row in self.slabs(part):
                @pl.when(self.core == c)
                def _(first=first, at=at, row=row, flipped=flipped):
                    self.s[k, first, at : at + 16, :128] = flipped[row : row + 16, :]

                @pl.when(self.core != c)
                def _(first=first, at=at, row=row, flipped=flipped):
                    self.other[i % 2, first, at : at + 16, :128] = flipped[row : row + 16, :]

    def sent(self, i):
        @pl.when(i >= SLOTS)
        def _():
            pl.semaphore_wait(self.credit, 1)

        self.start(0, i)

    def join_cores(self, i):
        self.wait(0, i)
        k = i % SLOTS
        for chunk in range(4):
            self.s[k, chunk] = self.s[k, chunk] + self.crecv[k, chunk]

        @pl.when(i + SLOTS < self.blocks)
        def _():
            pl.semaphore_signal(
                self.credit, inc=1, device_id={"dp": self.partner}, device_id_type=MESH
            )

        self.start(1, i)

    def first_ring(self, i):
        self.wait(1, i)
        s, k = self.s, i % SLOTS
        s[k, self.ap, :64] = s[k, self.ap, :64] + self.p1[i]
        s[k, self.am, 64:] = s[k, self.am, 64:] + self.m1[i]
        self.start(2, i)

    def first_done(self, i):
        self.wait(2, i)
        k = i % SLOTS
        for chunk in range(4):
            rows = pl.ds(chunk * 32, 32)
            self.t[k, chunk] = self.s[k, self.a, rows] + self.p2[i, rows] + self.m2[i, rows]
        self.start(3, i)

    def second_ring(self, i):
        self.wait(3, i)
        t, k = self.t, i % SLOTS
        t[k, self.bp, :16] = t[k, self.bp, :16] + self.q1[i]
        t[k, self.bm, 16:] = t[k, self.bm, 16:] + self.r1[i]
        self.start(4, i)

    def second_done(self, i):
        self.wait(4, i)
        k = i % SLOTS
        for chunk in range(2):
            rows = pl.ds(chunk * 16, 16)
            self.u[k, chunk] = self.t[k, self.b, rows] + self.q2[i, rows] + self.r2[i, rows]
        self.start(5, i)

    def share(self, i):
        self.wait(5, i)
        return self.u[i % SLOTS, self.zh] + self.zrecv[i]

    def run(self, make, finish, extra):
        def made(i):
            make(i)
            self.sent(i)

        stages = (
            made, self.join_cores, self.first_ring, self.first_done, self.second_ring, self.second_done,
            lambda i: finish(i, self.share(i)),
        )

        def step(j, carry):
            for stage, offset in zip(stages, OFFSETS):
                i = j - offset

                @pl.when((i >= 0) & (i < self.blocks))
                def _(stage=stage, i=i):
                    stage(i)

            extra(j)
            return carry

        lax.fori_loop(0, self.blocks + OFFSETS[-1], step, 0)


def cols_of(i, first):
    return pl.ds(pl.multiple_of((i - first) * W, W), W)


def at_step(cond):
    def wrap(f):
        pl.when(cond)(f)

    return wrap


def back_kernel(
    slopes, n2_ref, cot_ref, branch_ref, n1_ref, lse_ref, vec_two, up_sums, gain_ref,
    act_any, gh_any, att_any, q_any, k_any, v_any, wout_any, woth_any, wqkv_any, tokens_any, grad_any,
    down_out, up_out, out_out, qkv_out, vec_out, vec_late, sum_out, token_ref,
    distance, rbuf, q_v, k_v, v_v, wout, woth, wqkv, tokens, grad, ga, dq, dk, dv, small, every,
    rsems, lsem, gs, gr, *ring_refs,
):
    early = ((q_any, q_v), (k_any, k_v), (v_any, v_v), (wout_any, wout), (woth_any, woth))
    late = ((wqkv_any, wqkv), (tokens_any, tokens), (grad_any, grad))
    local = [
        pltpu.make_async_copy(src, dst, lsem.at[k]) for k, (src, dst) in enumerate(early + late)
    ]

    def right(kind, n):
        src = (act_any, gh_any)[kind]
        return pltpu.make_async_copy(src.at[:, cols_of(n, 4 * kind)], rbuf.at[n % 2], rsems.at[n % 2])

    right(0, 0).start()
    for c in local:
        c.start()
    att_copy = pltpu.make_async_copy(att_any.at[0], ga.at[0], rsems.at[2])
    ring = Ring(14, (4, 9), ring_refs)
    fill_distance(distance)
    ring.turn(cot_ref)
    ring.enter()
    core, a, b, zh = ring.core, ring.a, ring.b, ring.zh
    parts = (dq, dk, dv)

    def make(i):
        for first, left in ((5, n2_ref), (10, branch_ref), (11, n1_ref)):
            @pl.when(i == first)
            def _(left=left):
                ring.turn(left)

        for kind in range(2):
            first = 5 * kind

            @pl.when((i >= first) & (i < first + 4))
            def _(kind=kind):
                n = i - kind

                @pl.when(n < 3 + 4 * kind)
                def _():
                    right(kind, n + 1).start()

                if kind == 0:
                    @pl.when(n == 3)
                    def _():
                        right(1, n + 1).start()

                right(kind, n).wait()
                ring.make_product(i, rbuf[n % 2])

        @pl.when(i == 4)
        def _():
            small[...] = jnp.zeros_like(small)
            small[0:8, :] = vec_two[...]
            small[10:12, :] = up_sums[...]
            small[12:13, :512] = jnp.sum(dq[0].astype(f32), axis=0, keepdims=True)
            small[12:13, 512:] = jnp.sum(dv[0].astype(f32), axis=0, keepdims=True)

        @pl.when((i == 4) | (i == 9))
        def _():
            ring.make_small(i, small)

        @pl.when(i == 10)
        def _():
            att_copy.wait()
            ring.make_product(i, ga[0])

        for k in range(3):
            @pl.when(i == 11 + k)
            def _(k=k):
                ring.make_product(i, parts[k][0])

    def finish(i, share):
        for first, target in ((0, down_out), (5, up_out)):
            @pl.when((i >= first) & (i < first + 4))
            def _(first=first, target=target):
                target[:, cols_of(i, first)] = share

        @pl.when(i == 4)
        def _():
            vec_out[...] = share[:, :128]

        @pl.when(i == 9)
        def _():
            vec_late[...] = share[:, :128]

        @pl.when(i == 10)
        def _():
            out_out[...] = share

        @pl.when(i >= 11)
        def _():
            qkv_out[i - 11] = share

    def spread(number):
        mine = every.at[core]
        if number == 0:
            moves = [(0, mine.at[a, b, zh], ring.across)]
        elif number == 1:
            targets = (ring.to_bp, ring.to_bm, ring.to_b2)
            moves = [(k + 1, mine.at[a, b], d) for k, d in enumerate(targets)]
        elif number == 2:
            targets = (ring.to_ap, ring.to_am, ring.to_a2)
            moves = [(k + 4, mine.at[a], d) for k, d in enumerate(targets)]
        else:
            moves = [(7, mine, ring.partner)]
        return [
            pltpu.make_async_remote_copy(
                src_ref=place,
                dst_ref=place,
                send_sem=gs.at[k],
                recv_sem=gr.at[k],
                device_id={"dp": d},
                device_id_type=MESH,
            )
            for k, place, d in moves
        ]

    def spread_step(number):
        if number == 0:
            every[core, a, b, zh] = vec_out[...]
        else:
            for c in spread(number - 1):
                c.wait()
        if number < 4:
            for c in spread(number):
                c.start()
        else:
            for part in range(8):
                rows = [None] * 8
                for c, first, at, row in ring.slabs(part):
                    rows[row // 16] = every[c, first, at // 32, (at // 16) % 2]
                flipped = jnp.concatenate(rows, axis=0).T
                sum_out[:, part * 128 : (part + 1) * 128] = flipped[8:16]

    def extra(j):
        @pl.when(j == 0)
        def _():
            for c in local[:5]:
                c.wait()
            ga[0] = dot(branch_ref[...], wout[...], NT).astype(bf16)
            ga[1] = dot(branch_ref[...], woth[3], NT).astype(bf16)

        def one_pair(pair, carry):
            half, p = pair // 4, pair % 4
            lanes = pl.ds(pl.multiple_of(p * 128, 128), 128)
            lane = lax.broadcasted_iota(jnp.int32, lse_ref.shape, 1)
            lses = [
                jnp.sum(jnp.where(lane == 2 * pair + side, lse_ref[...], 0.0), axis=1, keepdims=True)
                for side in range(2)
            ]
            one, two, three = attend_back_pair(
                q_v[half, :, lanes],
                k_v[half, :, lanes],
                v_v[half, :, lanes],
                lses,
                ga[half, :, lanes],
                (slopes[2 * pair], slopes[2 * pair + 1]),
                distance,
            )
            dq[half, :, lanes] = one
            dk[half, :, lanes] = two
            dv[half, :, lanes] = three
            return carry

        @pl.when((j >= 1) & (j < 5))
        def _():
            lax.fori_loop(2 * j - 2, 2 * j, one_pair, 0)

        @pl.when(j == 4)
        def _():
            att_copy.start()

        for k in range(3):
            @pl.when(j == 5 + k)
            def _(k=k):
                if k == 0:
                    for c in local[5:]:
                        c.wait()
                one = dot(parts[k][0], wqkv[k], NT)
                two = dot(parts[k][1], woth[k])
                if k == 0:
                    token_ref[...] = one + two
                else:
                    token_ref[...] += one + two

        @pl.when(j == 8)
        def _():
            def rows_of(r, carry):
                rows = pl.ds(pl.multiple_of(r * 64, 64), 64)
                n, root = layer_norm_parts(tokens[rows, :].astype(f32))
                back, ggain, gshift = layer_norm_back(token_ref[rows, :], n, root, gain_ref[0:1, :])
                token_ref[rows, :] = grad[rows, :] + back
                small[8:9, :] += ggain[None]
                small[9:10, :] += gshift[None]
                return carry

            lax.fori_loop(0, 8, rows_of, 0)

        for number in range(5):
            @pl.when(j == 11 + number)
            def _(number=number):
                spread_step(number)

    ring.run(make, finish, extra)


def backward(slopes, n2, cot, branch, n1, lse, vec, up_sums, gain, act, gh, att, q, k, v, wout, woth, wqkv, tokens, grad):
    length, width = n1.shape
    vmem = pl.BlockSpec(memory_space=pltpu.VMEM)
    hbm = pl.BlockSpec(memory_space=pl.ANY)
    return pl.pallas_call(
        back_kernel,
        in_specs=[pl.BlockSpec(memory_space=pltpu.SMEM)] + [vmem] * 8 + [hbm] * 11,
        out_specs=[vmem] * 8,
        out_shape=[
            jax.ShapeDtypeStruct((16, 2048), f32),
            jax.ShapeDtypeStruct((16, 2048), f32),
            jax.ShapeDtypeStruct((16, 512), f32),
            jax.ShapeDtypeStruct((3, 16, 512), f32),
            jax.ShapeDtypeStruct((16, 128), f32),
            jax.ShapeDtypeStruct((16, 128), f32),
            jax.ShapeDtypeStruct((8, 1024), f32),
            jax.ShapeDtypeStruct((length, width), f32),
        ],
        scratch_shapes=[
            pltpu.VMEM((length, length), f32),
            pltpu.VMEM((2, length, W), bf16),
            pltpu.VMEM(q.shape, bf16),
            pltpu.VMEM(q.shape, bf16),
            pltpu.VMEM(q.shape, bf16),
            pltpu.VMEM(wout.shape, bf16),
            pltpu.VMEM(woth.shape, bf16),
            pltpu.VMEM(wqkv.shape, bf16),
            pltpu.VMEM(tokens.shape, bf16),
            pltpu.VMEM(grad.shape, f32),
            pltpu.VMEM(q.shape, bf16),
            pltpu.VMEM(q.shape, bf16),
            pltpu.VMEM(q.shape, bf16),
            pltpu.VMEM(q.shape, bf16),
            pltpu.VMEM((128, width), f32),
            pltpu.VMEM((2, 4, 4, 2, 16, 128), f32),
            pltpu.SemaphoreType.DMA((3,)),
            pltpu.SemaphoreType.DMA((8,)),
            pltpu.SemaphoreType.DMA((8,)),
            pltpu.SemaphoreType.DMA((8,)),
            *ring_scratch(14),
        ],
        compiler_params=pltpu.CompilerParams(
            collective_id=0, has_side_effects=True, vmem_limit_bytes=63 * 2**20
        ),
    )(slopes, n2, cot, branch, n1, lse, vec, up_sums, gain, act, gh, att, q, k, v, wout, woth, wqkv, tokens, grad)


def on_device(
    tokens,
    gain_one,
    shift_one,
    qkv_weight,
    qv_bias,
    out_weight,
    out_bias,
    gain_two,
    shift_two,
    up_weight,
    up_bias,
    down_weight,
    down_bias,
    cotangent,
):
    dp, tensor = lax.axis_index("dp"), lax.axis_index("tensor")
    core, x, y = dp % 2, (dp // 2) % 4, (dp // 8) % 4
    ring = jnp.where(core == 0, x, y)
    ring_other = jnp.where(core == 0, y, x)
    offsets = (0, 3, 1, 2)
    other_ids = [4 * core + (ring + o) % 4 for o in offsets]
    other_ids += [4 * (1 - core) + (ring_other + o) % 4 for o in offsets]

    own_heads = tensor * 8 + jnp.arange(8, dtype=jnp.int32)
    oth_heads = (1 - tensor) * 8 + jnp.stack(other_ids).astype(jnp.int32)
    slopes = jnp.exp2(-8.0 * (jnp.concatenate([own_heads, oth_heads]) + 1).astype(f32) / 16)
    rows = jnp.concatenate([gain_one, shift_one, gain_two, shift_two]).reshape(4, 1024)
    low_rows = jnp.concatenate(
        [out_bias, down_bias, up_bias, qv_bias[0], qv_bias[1], jnp.zeros((3072,), bf16)]
    ).reshape(8, 1024)
    wqkv = qkv_weight.transpose(1, 0, 2)
    (
        normed_one,
        queries,
        key_rows,
        values,
        attended,
        lse,
        woth,
        _,
        normed_two,
        active_own,
        gh_own,
        grad_up_bias,
        block_out,
        grad_middle,
        grad_branch,
        sums_two,
    ) = forward(
        slopes,
        tokens,
        rows,
        low_rows,
        wqkv,
        out_weight,
        up_weight,
        down_weight,
        cotangent,
    )
    share_down, share_up, share_out, share_qkv, vector, late, summed, token_grad = backward(
        slopes,
        normed_two,
        cotangent,
        grad_branch,
        normed_one,
        lse,
        sums_two,
        grad_up_bias,
        rows,
        active_own,
        gh_own,
        attended,
        queries,
        key_rows,
        values,
        out_weight,
        woth,
        wqkv,
        tokens,
        grad_middle,
    )
    return (
        block_out,
        token_grad,
        late[:, 8],
        late[:, 9],
        share_qkv.transpose(1, 0, 2),
        summed[4].reshape(2, 512),
        share_out.T,
        vector[:, 2],
        vector[:, 0],
        vector[:, 1],
        share_up,
        summed[2:4].reshape(2048),
        share_down.T,
        vector[:, 3],
    )


def solution(mesh):
    placed = (
        P("dp", None),
        P(),
        P(),
        P(None, None, "tensor"),
        P(None, "tensor"),
        P("tensor", None),
        P(),
        P(),
        P(),
        P(None, "tensor"),
        P("tensor"),
        P("tensor", None),
        P(),
        P("dp", None),
    )
    return jax.shard_map(
        on_device,
        mesh=mesh,
        in_specs=placed,
        out_specs=(
            P("dp", None),
            P("dp", None),
            P("dp"),
            P("dp"),
            P("dp", None, "tensor"),
            P(None, "tensor"),
            P("tensor", "dp"),
            P("dp"),
            P("dp"),
            P("dp"),
            P("dp", "tensor"),
            P("tensor"),
            P("tensor", "dp"),
            P("dp"),
        ),
        check_vma=False,
    )
```

profile of v0, /device:TPU:0, one launch (start us, length us, event | category | flops | bytes accessed | tf_op | source)
XLA Modules:
  0.0 226.3 jit_solution(14992055842896247002)
XLA Ops:
  0.8 0.1 stack.35
  0.9 0.6 fusion.2.slopes
  1.5 0.8 slice_reduce_fusion.7
  2.3 0.7 pad_maximum_fusion
  3.0 0.6 reshape.37.rows_ref.gain_ref
  3.7 0.7 constant_dynamic-update-slice_fusion.3
  4.3 0.7 constant_dynamic-update-slice_fusion.2
  5.0 0.7 constant_dynamic-update-slice_fusion.1
  5.7 0.2 dynamic-update-slice.3
  5.9 0.2 dynamic-update-slice.4
  6.1 0.6 reshape.38.low_rows
  6.7 97.9 %shard_map.245 = (bf16[512,1024]{1,0:T(8,128)(2,1)}, bf16[2,512,512]{2,1,0:T(8,128)(2,1)}, bf16[2,512,512]{2,1,0:T(8,128)(2,1)}, bf16[2,512,512]{2,1,0:T(8,128)(...) custom-call(f32[16]{0:T(128)} %fusion.2.slopes, ...), custom_call_target="tpu_custom_call" | custom-call | tf_op jit(solution)/shard_map/pallas_call | solution.py:501
  104.6 109.4 %shard_map.246 = (f32[16,2048]{1,0:T(8,128)}, f32[16,2048]{1,0:T(8,128)}, f32[16,512]{1,0:T(8,128)}, f32[3,16,512]{2,1,0:T(8,128)}, f32[16,128]{1,0:T(8,128)}, /...) custom-call(f32[16]{0:T(128)} %fusion.2.slopes, bf16[512,1024]{1,0:T(8,128)(2,1)} %get-tuple-element.38.n2_ref, ...), custom_call_target="tpu_custom_call" | custom-call | tf_op jit(solution)/shard_map/pallas_call | solution.py:1016
  214.0 0.0 copy-start
  214.0 1.6 slice_reduce_fusion.4
  215.6 1.6 slice_reduce_fusion
  217.2 0.8 slice_reduce_fusion.6
  217.9 0.8 slice_bitcast_fusion
  218.7 0.6 copy.30
  219.3 0.6 reshape_squeeze.3
  219.9 0.0 copy-start.3
  219.9 0.0 copy-start.4
  219.9 0.0 copy-start.2
  219.9 0.0 copy-start.1
  219.9 2.3 %copy.42 = bf16[512,1024]{1,0:T(8,128)(2,1)} copy(bf16[512,1024]{1,0:T(8,128)(2,1)} %get-tuple-element.84) | data formatting | bytes 2097152
  222.2 0.0 copy-done
  222.2 1.3 copy.43
  223.6 0.0 copy-done.3
  223.6 0.6 copy.44
  224.2 0.0 copy-done.4
  224.2 0.6 copy.45
  224.8 0.0 copy-done.2
  224.8 0.7 copy.46
  225.5 0.0 copy-done.1
  225.5 0.7 copy.47
  (2 shorter events, 0.0 us)
Async XLA Ops:
  214.0 8.2 %copy-start = (f32[512,1024]{1,0:T(8,128)S(1)}, f32[512,1024]{1,0:T(8,128)}, u32[]{:S(2)}) copy-start(f32[512,1024]{1,0:T(8,128)} %get-tuple-element.85) | copy-start | bytes 6291460
  219.9 3.6 %copy-start.3 = (f32[3,16,512]{2,1,0:T(8,128)S(1)}, f32[3,16,512]{2,1,0:T(8,128)}, u32[]{:S(2)}) copy-start(f32[3,16,512]{2,1,0:T(8,128)} %get-tuple-element.54) | copy-start | bytes 294916
  219.9 4.3 %copy-start.4 = (f32[16,512]{1,0:T(8,128)S(1)}, f32[16,512]{1,0:T(8,128)}, u32[]{:S(2)}) copy-start(f32[16,512]{1,0:T(8,128)} %get-tuple-element.56) | copy-start | bytes 98308
  219.9 4.9 %copy-start.2 = (f32[16,2048]{1,0:T(8,128)S(1)}, f32[16,2048]{1,0:T(8,128)}, u32[]{:S(2)}) copy-start(f32[16,2048]{1,0:T(8,128)} %get-tuple-element.94) | copy-start | bytes 393220
  219.9 5.6 %copy-start.1 = (f32[16,2048]{1,0:T(8,128)S(1)}, f32[16,2048]{1,0:T(8,128)}, u32[]{:S(2)}) copy-start(f32[16,2048]{1,0:T(8,128)} %get-tuple-element.59) | copy-start | bytes 393220
where the time goes:
time: 229 us; the launch traced here: 226 us
  Pallas kernels  207 us (90%)
  local copies, waits for them, and re-layouts  16.6 us (7%)
    pallas_call x1, Pallas kernels, backward(): pl.pallas_call(back_kernel, in_specs=[pl.BlockSpec(memory_space=pltpu.SME...  109 us
    pallas_call x1, Pallas kernels, forward(): pl.pallas_call(forward_kernel, in_specs=[pl.BlockSpec(memory_space=pltpu....  97.9 us
    unnamed x23, local copies, waits for them, and re-layouts  10 us

commit v1 on v0

--- a/solution.py
+++ b/solution.py
@@ -557,8 +557,8 @@
 
 
 W = 512
-OFFSETS = (0, 1, 2, 3, 4, 5, 6)
-SLOTS = 4
+OFFSETS = (0, 1, 2, 4, 5, 6, 7)
+SLOTS = 5
 
 
 def ring_scratch(nb):
@@ -1002,7 +1002,7 @@
             lax.fori_loop(0, 8, rows_of, 0)
 
         for number in range(5):
-            @pl.when(j == 11 + number)
+            @pl.when(j == 12 + number)
             def _(number=number):
                 spread_step(number)
 

time: 229 us -> 224 us (0.978)
  Pallas kernels: 207 us -> 202 us
    pallas_call x1, Pallas kernels: 109 us -> 104 us  [backward(): pl.pallas_call(back_kernel, in_specs=[pl.BlockSpec(memory_space=pltpu.SME...]
where the time goes in v1:
time: 224 us; the launch traced here: 221 us
  Pallas kernels  202 us (90%)
  local copies, waits for them, and re-layouts  16.6 us (7%)
    pallas_call x1, Pallas kernels, backward(): pl.pallas_call(back_kernel, in_specs=[pl.BlockSpec(memory_space=pltpu.SME...  104 us
    pallas_call x1, Pallas kernels, forward(): pl.pallas_call(forward_kernel, in_specs=[pl.BlockSpec(memory_space=pltpu....  97.9 us
    unnamed x23, local copies, waits for them, and re-layouts  10 us

profile of v1, /device:TPU:0, one launch (start us, length us, event | category | flops | bytes accessed | tf_op | source)
XLA Modules:
  0.0 221.4 jit_solution(16482212128219338210)
XLA Ops:
  0.8 0.1 stack.35
  0.9 0.6 fusion.2.slopes
  1.5 0.8 slice_reduce_fusion.7
  2.3 0.7 pad_maximum_fusion
  3.0 0.6 reshape.37.rows_ref.gain_ref
  3.7 0.7 constant_dynamic-update-slice_fusion.3
  4.3 0.7 constant_dynamic-update-slice_fusion.2
  5.0 0.7 constant_dynamic-update-slice_fusion.1
  5.7 0.2 dynamic-update-slice.3
  5.9 0.2 dynamic-update-slice.4
  6.1 0.6 reshape.38.low_rows
  6.7 97.9 %shard_map.245 = (bf16[512,1024]{1,0:T(8,128)(2,1)}, bf16[2,512,512]{2,1,0:T(8,128)(2,1)}, bf16[2,512,512]{2,1,0:T(8,128)(2,1)}, bf16[2,512,512]{2,1,0:T(8,128)(...) custom-call(f32[16]{0:T(128)} %fusion.2.slopes, ...), custom_call_target="tpu_custom_call" | custom-call | tf_op jit(solution)/shard_map/pallas_call | solution.py:501
  104.6 104.5 %shard_map.246 = (f32[16,2048]{1,0:T(8,128)}, f32[16,2048]{1,0:T(8,128)}, f32[16,512]{1,0:T(8,128)}, f32[3,16,512]{2,1,0:T(8,128)}, f32[16,128]{1,0:T(8,128)}, /...) custom-call(f32[16]{0:T(128)} %fusion.2.slopes, bf16[512,1024]{1,0:T(8,128)(2,1)} %get-tuple-element.38.n2_ref, ...), custom_call_target="tpu_custom_call" | custom-call | tf_op jit(solution)/shard_map/pallas_call | solution.py:1016
  209.1 0.0 copy-start
  209.1 1.6 slice_reduce_fusion.4
  210.7 1.6 slice_reduce_fusion
  212.2 0.8 slice_reduce_fusion.6
  213.0 0.8 slice_bitcast_fusion
  213.8 0.6 copy.30
  214.4 0.6 reshape_squeeze.3
  215.0 0.0 copy-start.3
  215.0 0.0 copy-start.4
  215.0 0.0 copy-start.2
  215.0 0.0 copy-start.1
  215.0 2.3 %copy.42 = bf16[512,1024]{1,0:T(8,128)(2,1)} copy(bf16[512,1024]{1,0:T(8,128)(2,1)} %get-tuple-element.84) | data formatting | bytes 2097152
  217.3 0.0 copy-done
  217.3 1.3 copy.43
  218.6 0.0 copy-done.3
  218.6 0.6 copy.44
  219.3 0.0 copy-done.4
  219.3 0.6 copy.45
  219.9 0.0 copy-done.2
  219.9 0.7 copy.46
  220.5 0.0 copy-done.1
  220.6 0.7 copy.47
  (2 shorter events, 0.0 us)
Async XLA Ops:
  209.1 8.2 %copy-start = (f32[512,1024]{1,0:T(8,128)S(1)}, f32[512,1024]{1,0:T(8,128)}, u32[]{:S(2)}) copy-start(f32[512,1024]{1,0:T(8,128)} %get-tuple-element.85) | copy-start | bytes 6291460
  215.0 3.6 %copy-start.3 = (f32[3,16,512]{2,1,0:T(8,128)S(1)}, f32[3,16,512]{2,1,0:T(8,128)}, u32[]{:S(2)}) copy-start(f32[3,16,512]{2,1,0:T(8,128)} %get-tuple-element.54) | copy-start | bytes 294916
  215.0 4.3 %copy-start.4 = (f32[16,512]{1,0:T(8,128)S(1)}, f32[16,512]{1,0:T(8,128)}, u32[]{:S(2)}) copy-start(f32[16,512]{1,0:T(8,128)} %get-tuple-element.56) | copy-start | bytes 98308
  215.0 4.9 %copy-start.2 = (f32[16,2048]{1,0:T(8,128)S(1)}, f32[16,2048]{1,0:T(8,128)}, u32[]{:S(2)}) copy-start(f32[16,2048]{1,0:T(8,128)} %get-tuple-element.94) | copy-start | bytes 393220
  215.0 5.6 %copy-start.1 = (f32[16,2048]{1,0:T(8,128)S(1)}, f32[16,2048]{1,0:T(8,128)}, u32[]{:S(2)}) copy-start(f32[16,2048]{1,0:T(8,128)} %get-tuple-element.59) | copy-start | bytes 393220

commit v2 on v1

--- a/solution.py
+++ b/solution.py
@@ -557,8 +557,8 @@
 
 
 W = 512
-OFFSETS = (0, 1, 2, 4, 5, 6, 7)
-SLOTS = 5
+OFFSETS = (0, 1, 3, 5, 6, 7, 8)
+SLOTS = 6
 
 
 def ring_scratch(nb):
@@ -1002,7 +1002,7 @@
             lax.fori_loop(0, 8, rows_of, 0)
 
         for number in range(5):
-            @pl.when(j == 12 + number)
+            @pl.when(j == 13 + number)
             def _(number=number):
                 spread_step(number)
 

time: 224 us -> 226 us (level)
  no operation moved by 1% of the time
where the time goes in v2:
time: 226 us; the launch traced here: 223 us
  Pallas kernels  203 us (90%)
  local copies, waits for them, and re-layouts  16.6 us (7%)
    pallas_call x1, Pallas kernels, backward(): pl.pallas_call(back_kernel, in_specs=[pl.BlockSpec(memory_space=pltpu.SME...  106 us
    pallas_call x1, Pallas kernels, forward(): pl.pallas_call(forward_kernel, in_specs=[pl.BlockSpec(memory_space=pltpu....  97.9 us
    unnamed x23, local copies, waits for them, and re-layouts  10 us

profile of v2, /device:TPU:0, one launch (start us, length us, event | category | flops | bytes accessed | tf_op | source)
XLA Modules:
  0.0 222.5 jit_solution(4488938386621502571)
XLA Ops:
  0.8 0.1 stack.35
  0.9 0.6 fusion.2.slopes
  1.5 0.8 slice_reduce_fusion.7
  2.3 0.7 pad_maximum_fusion
  3.0 0.6 reshape.37.rows_ref.gain_ref
  3.7 0.7 constant_dynamic-update-slice_fusion.3
  4.3 0.7 constant_dynamic-update-slice_fusion.2
  5.0 0.7 constant_dynamic-update-slice_fusion.1
  5.7 0.2 dynamic-update-slice.3
  5.9 0.2 dynamic-update-slice.4
  6.1 0.6 reshape.38.low_rows
  6.7 97.9 %shard_map.245 = (bf16[512,1024]{1,0:T(8,128)(2,1)}, bf16[2,512,512]{2,1,0:T(8,128)(2,1)}, bf16[2,512,512]{2,1,0:T(8,128)(2,1)}, bf16[2,512,512]{2,1,0:T(8,128)(...) custom-call(f32[16]{0:T(128)} %fusion.2.slopes, ...), custom_call_target="tpu_custom_call" | custom-call | tf_op jit(solution)/shard_map/pallas_call | solution.py:501
  104.6 105.6 %shard_map.246 = (f32[16,2048]{1,0:T(8,128)}, f32[16,2048]{1,0:T(8,128)}, f32[16,512]{1,0:T(8,128)}, f32[3,16,512]{2,1,0:T(8,128)}, f32[16,128]{1,0:T(8,128)}, /...) custom-call(f32[16]{0:T(128)} %fusion.2.slopes, bf16[512,1024]{1,0:T(8,128)(2,1)} %get-tuple-element.38.n2_ref, ...), custom_call_target="tpu_custom_call" | custom-call | tf_op jit(solution)/shard_map/pallas_call | solution.py:1016
  210.2 0.0 copy-start
  210.2 1.6 slice_reduce_fusion.4
  211.8 1.6 slice_reduce_fusion
  213.4 0.8 slice_reduce_fusion.6
  214.2 0.8 slice_bitcast_fusion
  214.9 0.6 copy.30
  215.5 0.6 reshape_squeeze.3
  216.1 0.0 copy-start.3
  216.1 0.0 copy-start.4
  216.1 0.0 copy-start.2
  216.1 0.0 copy-start.1
  216.1 2.3 %copy.42 = bf16[512,1024]{1,0:T(8,128)(2,1)} copy(bf16[512,1024]{1,0:T(8,128)(2,1)} %get-tuple-element.84) | data formatting | bytes 2097152
  218.4 0.0 copy-done
  218.5 1.3 copy.43
  219.8 0.0 copy-done.3
  219.8 0.6 copy.44
  220.4 0.0 copy-done.4
  220.4 0.6 copy.45
  221.0 0.0 copy-done.2
  221.0 0.7 copy.46
  221.7 0.0 copy-done.1
  221.7 0.7 copy.47
  (2 shorter events, 0.0 us)
Async XLA Ops:
  210.2 8.2 %copy-start = (f32[512,1024]{1,0:T(8,128)S(1)}, f32[512,1024]{1,0:T(8,128)}, u32[]{:S(2)}) copy-start(f32[512,1024]{1,0:T(8,128)} %get-tuple-element.85) | copy-start | bytes 6291460
  216.1 3.6 %copy-start.3 = (f32[3,16,512]{2,1,0:T(8,128)S(1)}, f32[3,16,512]{2,1,0:T(8,128)}, u32[]{:S(2)}) copy-start(f32[3,16,512]{2,1,0:T(8,128)} %get-tuple-element.54) | copy-start | bytes 294916
  216.1 4.3 %copy-start.4 = (f32[16,512]{1,0:T(8,128)S(1)}, f32[16,512]{1,0:T(8,128)}, u32[]{:S(2)}) copy-start(f32[16,512]{1,0:T(8,128)} %get-tuple-element.56) | copy-start | bytes 98308
  216.1 4.9 %copy-start.2 = (f32[16,2048]{1,0:T(8,128)S(1)}, f32[16,2048]{1,0:T(8,128)}, u32[]{:S(2)}) copy-start(f32[16,2048]{1,0:T(8,128)} %get-tuple-element.94) | copy-start | bytes 393220
  216.1 5.6 %copy-start.1 = (f32[16,2048]{1,0:T(8,128)S(1)}, f32[16,2048]{1,0:T(8,128)}, u32[]{:S(2)}) copy-start(f32[16,2048]{1,0:T(8,128)} %get-tuple-element.59) | copy-start | bytes 393220
